TPU v7x, 32 devices: a whole 2x2x4 slice. The times are simulated.
32 devices in a mesh: groups: 2 (over y), wide: 4 (over z), narrow: 4 (over x, core).
Axes of the slice: x: 2, y: 2, z: 4, core: 2. Of those that a mesh axis runs over, the one named last changes fastest.
Arguments:
- projected: bfloat16 [3, 512, 2048], P(None, ('groups', 'wide', 'narrow')), parts along dimension 1, may hold values from -6 to 6
- latents: bfloat16 [512, 2048], P(('groups', 'wide', 'narrow')), parts along dimension 0, may hold values from -6 to 6
- modulation: float32 [8, 2048], P('groups'), parts along dimension 0, may hold values from -3 to 3
- routes: int32 [512, 2], P(('groups', 'wide')), parts along dimension 0, may hold values from 0 to 7, all different within a row; in each aligned block of 64 rows (0 to 63, 64 to 127, ...) at most 24 rows name the same one
- route_weights: float32 [512, 2], P(('groups', 'wide')), parts along dimension 0, may hold values from 0.2 to 1
- out_proj: bfloat16 [2048, 2048], P('narrow'), may hold values from -0.75 to 0.75
- expert_up: bfloat16 [8, 2048, 4096], P('wide', None, 'narrow'), may hold values from -0.125 to 0.125
- expert_down: bfloat16 [8, 4096, 2048], P('wide', 'narrow'), may hold values from -0.09375 to 0.09375
Outputs:
- updated: bfloat16 [512, 2048], P(('groups', 'wide', 'narrow')), parts along dimension 0
There are 2 independent parts, one for each index of `groups`. A program takes and returns all parts, laid end to end along the dimension named above; an argument that names none is the same for every part. Nothing has to cross between parts.
Inputs may be any that keep to these rules, and one draw needn't show every extreme that they name: `routes`: each row names two different experts. In each aligned block of 64 rows no expert is named by more than 24 rows, and in every draw some expert is named by exactly 24 rows of some block.
All inputs are finite; a program needn't handle non-finite values.
Results may differ from a plain program's by a relative error of at most 0.012.
Values may be sent and summed in bfloat16 or wider, within the bound.
A program may use at most 64 MiB of HBM per device.

v0:
```python
import jax
import jax.numpy as jnp
from jax import lax
from jax.sharding import PartitionSpec as P

HEAD_DIM = 64


EPSILON = 1e-06


def slot_numbers(route_block, expert_count, most_rows):
    flat_routes = route_block.reshape(-1)
    onehot_table = (
        flat_routes[:, None] == jnp.arange(expert_count, dtype=jnp.int32)[None, :]
    ).astype(jnp.int32)
    earlier = jnp.cumsum(onehot_table, axis=0, dtype=jnp.int32) - onehot_table
    position = jnp.sum(earlier * onehot_table, axis=1, dtype=jnp.int32)
    return flat_routes * most_rows + position


def on_device(
    projected, latents, modulation, routes, route_weights, out_proj, expert_up, expert_down
):
    tok_dev = latents.shape[0]
    model_width = latents.shape[1]
    narrow_count = lax.axis_size("narrow")
    wide_count = lax.axis_size("wide")
    narrow_index = lax.axis_index("narrow")
    shard_rows = tok_dev * narrow_count
    local_width = out_proj.shape[0]
    local_heads = local_width // HEAD_DIM
    regrouped = lax.all_to_all(projected, "narrow", split_axis=2, concat_axis=1, tiled=True)
    queries = regrouped[0].reshape(shard_rows, local_heads, HEAD_DIM)
    scale_factor = HEAD_DIM ** (-0.5)
    row_max = jnp.full((shard_rows, local_heads), -1e30, jnp.float32)
    key_rows = lax.all_gather(regrouped[1], "wide", axis=0, tiled=True).reshape(
        -1, local_heads, HEAD_DIM
    )
    value_rows = lax.all_gather(regrouped[2], "wide", axis=0, tiled=True).reshape(
        -1, local_heads, HEAD_DIM
    )
    scores = (
        jnp.einsum("qhd,khd->qhk", queries, key_rows, preferred_element_type=jnp.float32)
        * scale_factor
    )
    new_max = jnp.maximum(row_max, jnp.max(scores, axis=2))
    weights = jnp.exp(scores - new_max[:, :, None])
    new_total = jnp.sum(weights, axis=2)
    new_accum = jnp.einsum(
        "qhk,khd->qhd", weights.astype(jnp.bfloat16), value_rows, preferred_element_type=jnp.float32
    )
    attended = (
        (new_accum / new_total[:, :, None]).astype(jnp.bfloat16).reshape(shard_rows, local_width)
    )
    branch = lax.psum_scatter(
        jnp.dot(attended, out_proj, preferred_element_type=jnp.float32).astype(jnp.bfloat16),
        "narrow",
        scatter_dimension=0,
        tiled=True,
    ).astype(jnp.float32)
    residual = latents.astype(jnp.float32) + modulation[0][None, :] * branch
    mean_value = jnp.mean(residual, axis=1, keepdims=True)
    centered = residual - mean_value
    variance = jnp.mean(centered * centered, axis=1, keepdims=True)
    normed = centered * lax.rsqrt(variance + EPSILON)
    expert_in = (normed * (1.0 + modulation[2][None, :]) + modulation[1][None, :]).astype(
        jnp.bfloat16
    )
    shard_in = lax.all_gather(expert_in, "narrow", axis=0, tiled=True)
    exp_dev = expert_up.shape[0]
    experts_all = exp_dev * wide_count
    most_rows = 3 * tok_dev * narrow_count // experts_all
    column_slots = exp_dev * most_rows
    slot_ids = slot_numbers(routes, experts_all, most_rows)
    token_ids = jnp.arange(2 * shard_rows, dtype=jnp.int32) // 2
    slot_table = jnp.full((experts_all * most_rows,), -1, jnp.int32).at[slot_ids].set(token_ids)
    taken_rows = shard_in[jnp.maximum(slot_table, 0)]
    bucket = jnp.where(slot_table[:, None] >= 0, taken_rows, jnp.zeros_like(taken_rows)).reshape(
        wide_count, column_slots, model_width
    )
    arrived = lax.all_to_all(bucket, "wide", split_axis=0, concat_axis=0, tiled=True)
    sources = arrived.shape[0]
    grouped = arrived.reshape(sources, exp_dev, most_rows, model_width)
    hidden_units = jax.nn.gelu(
        jnp.einsum("sjmd,jdf->sjmf", grouped, expert_up, preferred_element_type=jnp.float32),
        approximate=True,
    ).astype(jnp.bfloat16)
    partial_rows = jnp.einsum(
        "sjmf,jfd->sjmd", hidden_units, expert_down, preferred_element_type=jnp.float32
    )
    summed = lax.psum(
        partial_rows.reshape(sources, column_slots, model_width).astype(jnp.bfloat16), "narrow"
    )
    returned = lax.all_to_all(summed, "wide", split_axis=0, concat_axis=0, tiled=True)
    flat_returned = returned.reshape(experts_all * most_rows, model_width)
    own_slots = lax.dynamic_slice_in_dim(
        slot_ids.reshape(shard_rows, 2), narrow_index * tok_dev, tok_dev, 0
    )
    own_weights = lax.dynamic_slice_in_dim(route_weights, narrow_index * tok_dev, tok_dev, 0)
    picked = flat_returned[own_slots]
    mixture = jnp.sum(own_weights[:, :, None] * picked.astype(jnp.float32), axis=1)
    updated = residual + modulation[3][None, :] * mixture
    return updated.astype(jnp.bfloat16)


def solution(mesh):
    in_specs = (
        P(None, ("groups", "wide", "narrow"), None),
        P(("groups", "wide", "narrow"), None),
        P("groups", None),
        P(("groups", "wide"), None),
        P(("groups", "wide"), None),
        P("narrow", None),
        P("wide", None, "narrow"),
        P("wide", "narrow", None),
    )
    out_specs = P(("groups", "wide", "narrow"), None)
    return jax.shard_map(
        on_device, mesh=mesh, in_specs=in_specs, out_specs=out_specs, check_vma=False
    )
```

profile of v0, /device:TPU:0, one launch (start us, length us, event | category | flops | bytes accessed | tf_op | source)
XLA Modules:
  0.0 195.1 jit_solution(12563853481658741717)
XLA Ops:
  6.5 3.9 %copy.35 = bf16[3,16,2048]{1,0,2:T(4,128)(2,1)} copy(bf16[3,16,2048]{2,1,0:T(8,128)(2,1)} %param.8) | data formatting | bytes 393216 | tf_op args[0]
  10.4 4.3 %reshape.118 = bf16[4,2,12288]{2,1,0:T(2,128)(2,1)} reshape(bf16[2048,3,16]{2,1,0:T(4,128)(2,1)} %bitcast.69) | data formatting | bytes 393216
  14.7 4.2 %all-to-all-start = ((bf16[4,2,12288]{2,1,0:T(2,128)(2,1)}), bf16[4,2,12288]{2,1,0:T(2,128)(2,1)S(1)}, u32[]{:S(2)}, u32[]{:S(2)}) async-start(bf16[4,2,12288]{2,1,0:T(2,128)(2,1)} %reshape.118), calls=%async_computation | async-start | bytes 393216 | tf_op jit(solution)/shard_map/all_to_all | solution.py:33
  19.0 0.8 copy.45
  20.0 0.2 reduce_window_sum.11
  20.2 0.2 select_reduce_fusion
  20.5 1.0 scatter_custom_fusion
  21.6 2.7 %all-to-all-done = bf16[4,2,12288]{2,1,0:T(2,128)(2,1)S(1)} async-done(((bf16[4,2,12288]{2,1,0:T(2,128)(2,1)}), bf16[4,2,12288]{2,1,0:T(2,128)(2,1)S(1)}, u32[]{:S(2)}, u32[]{:S(2)}) %all-to-all-start) | async-done | bytes 196640 | tf_op jit(solution)/shard_map/all_to_all | solution.py:33
  24.3 3.1 %reshape.119 = bf16[2048,3,16]{2,1,0:T(4,128)(2,1)} reshape(bf16[4,2,12288]{2,1,0:T(2,128)(2,1)S(1)} %all-to-all-done) | data formatting | bytes 393216
  27.3 3.0 %copy.51 = bf16[3,16,4,512]{3,2,1,0:T(4,128)(2,1)S(1)} copy(bf16[3,16,4,512]{1,0,3,2:T(4,128)(2,1)} %bitcast.68) | data formatting | bytes 393216 | tf_op jit(solution)/shard_map/all_to_all | solution.py:33
  30.5 14.6 %all_gather.9 = bf16[256,512]{1,0:T(8,128)(2,1)S(1)} all-gather(bf16[64,512]{1,0:T(8,128)(2,1)S(1)} %bitcast.76), channel_id=1, replica_groups=mesh['groups'=2,'wide'=4,'narrow'=4] {'wide'}, dimensions={0}, use_global_device_ids=true | all-gather | bytes 327680 | tf_op jit(solution)/shard_map/all_gather | solution.py:37
  45.4 0.3 fusion.49
  45.8 14.6 %all_gather.10 = bf16[256,512]{1,0:T(8,128)(2,1)S(1)} all-gather(bf16[64,512]{1,0:T(8,128)(2,1)S(1)} %bitcast.77), channel_id=1, replica_groups=mesh['groups'=2,'wide'=4,'narrow'=4] {'wide'}, dimensions={0}, use_global_device_ids=true | all-gather | bytes 327680 | tf_op jit(solution)/shard_map/all_gather | solution.py:40
  60.5 0.3 fusion.29
  60.8 0.3 fusion.15
  61.3 1.2 convolution_convert_fusion
  62.6 20.1 %reduce-scatter.2.cloned.1.call-done = bf16[16,2048]{1,0:T(8,128)(2,1)} async-done(((bf16[64,2048]{1,0:T(8,128)(2,1)}), bf16[16,2048]{1,0:T(8,128)(2,1)}) %reduce-scatter.2.cloned.1.call-update) | async-done | bytes 65552 | tf_op jit(solution)/shard_map/reduce_scatter | solution.py:56
  82.7 1.0 fusion.38
  83.7 1.0 multiply_reduce_fusion.1
  84.7 0.9 add_convert_fusion.1
  85.7 5.8 %all_gather.11 = bf16[64,2048]{1,0:T(8,128)(2,1)S(1)} all-gather(bf16[16,2048]{1,0:T(8,128)(2,1)S(1)} %add_convert_fusion.1), channel_id=1, replica_groups=mesh['groups'=2,'wide'=4,'narrow'=4] {'narrow'}, dimensions={0}, use_global_device_ids=true | all-gather | bytes 327680 | tf_op jit(solution)/shard_map/all_gather | solution.py:70
  91.5 1.1 gather_fusion
  92.7 25.0 %all_to_all.25 = bf16[4,48,2048]{2,1,0:T(8,128)(2,1)S(1)} all-to-all(bf16[4,48,2048]{2,1,0:T(8,128)(2,1)S(1)} %broadcast_select_fusion), channel_id=1, replica_groups=mesh['groups'=2,'wide'=4,'narrow'=4] {'wide'}, dimensions={0} | all-to-all | bytes 1572864 | tf_op jit(solution)/shard_map/all_to_all | solution.py:82
  117.8 9.7 %fusion.7 = bf16[4,2,24,2048]{3,2,0,1:T(8,128)(2,1)} fusion(bf16[2,1024,2048]{2,1,0:T(8,128)(2,1)} %param.15, bf16[2,2048,1024]{2,1,0:T(8,128)(2,1)} %param.14, bf16[4,2,24,2048]{3,2,1,0:T(8,128)(2,1)S(1)} %bitcast.70), kind=kOutput, calls=%fused_computation.8 | convolution fusion | flops 1612775424 | bytes 18350080 | tf_op jit(solution)/shard_map/sjmf,jfd->sjmd/dot_general | solution.py:89
  127.5 2.1 %copy.48 = bf16[4,2,24,2048]{3,2,1,0:T(8,128)(2,1)} copy(bf16[4,2,24,2048]{3,2,0,1:T(8,128)(2,1)} %fusion.7) | data formatting | bytes 1572864 | tf_op jit(solution)/shard_map/convert_element_type | solution.py:93
  129.6 32.9 %all-reduce.2.cloned.1.call-done = bf16[4,48,2048]{2,1,0:T(8,128)(2,1)} async-done(((bf16[4,48,2048]{2,1,0:T(8,128)(2,1)}), bf16[4,48,2048]{2,1,0:T(8,128)(2,1)}) %all-reduce.2.cloned.1.call-update) | async-done | bytes 786448 | tf_op jit(solution)/shard_map/psum | solution.py:92
  162.5 4.6 %all-to-all-start.2 = ((bf16[4,48,2048]{2,1,0:T(8,128)(2,1)}), bf16[4,48,2048]{2,1,0:T(8,128)(2,1)S(1)}, u32[]{:S(2)}, u32[]{:S(2)}) async-start(bf16[4,48,2048]{2,1,0:T(8,128)(2,1)} %all-reduce.2.cloned.1.call-done), calls=%async_computation.3 | async-start | bytes 1572864 | tf_op jit(solution)/shard_map/all_to_all | solution.py:95
  167.5 18.8 %all-to-all-done.2 = bf16[4,48,2048]{2,1,0:T(8,128)(2,1)S(1)} async-done(((bf16[4,48,2048]{2,1,0:T(8,128)(2,1)}), bf16[4,48,2048]{2,1,0:T(8,128)(2,1)S(1)}, u32[]{:S(2)}, u32[]{:S(2)}) %all-to-all-start.2) | async-done | bytes 786464 | tf_op jit(solution)/shard_map/all_to_all | solution.py:95
  186.4 0.6 gather_fusion.1
  187.0 0.2 reshape.113
  187.2 0.4 multiply_reduce_fusion
  187.6 0.7 add_convert_fusion
  (44 shorter events, 1.9 us)
Async XLA Ops:
  6.5 54.8 %copy-start = (bf16[512,2048]{1,0:T(8,128)(2,1)S(1)}, bf16[512,2048]{1,0:T(8,128)(2,1)}, u32[]{:S(2)}) copy-start(bf16[512,2048]{1,0:T(8,128)(2,1)} %param.13) | copy-start | bytes 6291460
  10.4 52.1 %copy-start.3 = (f32[4,2048]{1,0:T(4,128)S(1)}, f32[4,2048]{1,0:T(4,128)}, u32[]{:S(2)}) copy-start(f32[4,2048]{1,0:T(4,128)} %param.10) | copy-start | bytes 98308
  10.4 72.3 %copy-start.1 = (bf16[16,2048]{1,0:T(8,128)(2,1)S(1)}, bf16[16,2048]{1,0:T(8,128)(2,1)}, u32[]{:S(2)}) copy-start(bf16[16,2048]{1,0:T(8,128)(2,1)} %param.9) | copy-start | bytes 196612
  14.7 9.5 %all-to-all-start = ((bf16[4,2,12288]{2,1,0:T(2,128)(2,1)}), bf16[4,2,12288]{2,1,0:T(2,128)(2,1)S(1)}, u32[]{:S(2)}, u32[]{:S(2)}) async-start(bf16[4,2,12288]{2,1,0:T(2,128)(2,1)} %reshape.118), calls=%async_computation | async-start | bytes 393216 | tf_op jit(solution)/shard_map/all_to_all | solution.py:33
  19.0 63.7 %reduce-scatter.2.cloned.1.call-start = ((), (), s32[]{:S(2)}) async-start(), calls=%async_computation.4 | async-start | bytes 327680 | tf_op jit(solution)/shard_map/reduce_scatter | solution.py:56
  62.5 100.0 %all-reduce.2.cloned.1.call-start = ((), (), s32[]{:S(2)}) async-start(), calls=%async_computation.5 | async-start | bytes 1572864 | tf_op jit(solution)/shard_map/psum | solution.py:92
  117.8 49.6 %copy-start.4 = (f32[64,2]{0,1:T(2,128)S(1)}, f32[64,2]{0,1:T(2,128)}, u32[]{:S(2)}) copy-start(f32[64,2]{0,1:T(2,128)} %param.12) | copy-start | bytes 1540
  117.8 69.8 %copy-start.2 = (bf16[16,2048]{1,0:T(8,128)(2,1)S(1)}, bf16[16,2048]{1,0:T(8,128)(2,1)}, u32[]{:S(2)}) copy-start(bf16[16,2048]{1,0:T(8,128)(2,1)} %reduce-scatter.2.cloned.1.call-done) | copy-start | bytes 196612
  162.5 23.9 %all-to-all-start.2 = ((bf16[4,48,2048]{2,1,0:T(8,128)(2,1)}), bf16[4,48,2048]{2,1,0:T(8,128)(2,1)S(1)}, u32[]{:S(2)}, u32[]{:S(2)}) async-start(bf16[4,48,2048]{2,1,0:T(8,128)(2,1)} %all-reduce.2.cloned.1.call-done), calls=%async_computation.3 | async-start | bytes 1572864 | tf_op jit(solution)/shard_map/all_to_all | solution.py:95
Sparse Core Ops, SparseCore 0:
  62.6 20.0 reduce-scatter.1
  129.7 32.7 all-reduce.1
where the time goes:
time: 196 us; the launch traced here: 195 us
  waiting for transfers between devices  74.6 us (38%)
  blocking collectives  60 us (31%)
  local copies, waits for them, and re-layouts  21.6 us (11%)
  between operations  13.7 us (7%)
  matrix products  11.5 us (6%)
  starting transfers between devices  8.85 us (5%)
  other arithmetic  4.91 us (3%)
    psum x1, waiting for transfers between devices, on_device(): lax.psum(partial_rows.reshape(sources, column_slots, model_width).astype(...  32.9 us
    all_to_all x1, blocking collectives, on_device(): lax.all_to_all(bucket, 'wide', split_axis=0, concat_axis=0, tiled=True)  25 us
    reduce_scatter x1, waiting for transfers between devices, on_device(): lax.psum_scatter(jnp.dot(attended, out_proj, preferred_element_type=jnp.f...  20.1 us
    all_to_all x1, waiting for transfers between devices, on_device(): lax.all_to_all(summed, 'wide', split_axis=0, concat_axis=0, tiled=True)  18.8 us
    all_gather x1, blocking collectives, on_device(): lax.all_gather(regrouped[1], 'wide', axis=0, tiled=True)  14.6 us
    all_gather x1, blocking collectives, on_device(): lax.all_gather(regrouped[2], 'wide', axis=0, tiled=True)  14.6 us
    unnamed x14, local copies, waits for them, and re-layouts  12 us
    dot_general x1, matrix products, on_device(): jnp.einsum('sjmf,jfd->sjmd', hidden_units, expert_down, preferred_element...  9.71 us
  transfers between devices with their start and end apart: 4, of which 4 were waited for; matrix products, arithmetic and copies ran while one was open for 2% of the time, Pallas kernels for 0%

commit v1 on v0

--- a/solution.py
+++ b/solution.py
@@ -1,6 +1,9 @@
+import functools
 import jax
 import jax.numpy as jnp
 from jax import lax
+from jax.experimental import pallas as pl
+from jax.experimental.pallas import tpu as pltpu
 from jax.sharding import PartitionSpec as P
 
 HEAD_DIM = 64
@@ -104,6 +107,409 @@
     return updated.astype(jnp.bfloat16)
 
 
+def copy_to(source, target, sent, landed, device):
+    return pltpu.make_async_remote_copy(
+        src_ref=source,
+        dst_ref=target,
+        send_sem=sent,
+        recv_sem=landed,
+        device_id=device,
+        device_id_type=pl.DeviceIdType.MESH,
+    )
+
+
+def block_kernel(
+    wides,
+    chunks,
+    proj,
+    latents,
+    modulation,
+    table,
+    out_proj_hbm,
+    up_hbm,
+    down_hbm,
+    out,
+    out_proj,
+    up,
+    down,
+    qkv,
+    att,
+    att_all,
+    part,
+    part_all,
+    res,
+    rows,
+    gates,
+    hidden,
+    mixed,
+    core_in,
+    pair,
+    x_in,
+    quad,
+    z_in,
+    own_sem,
+    q_sent,
+    q_land,
+    t_sent,
+    t_land,
+    a_sent,
+    a_land,
+    b_sent,
+    b_land,
+    z_sent,
+    z_land,
+    x_sent,
+    x_land,
+    c_sent,
+    c_land,
+    d_sent,
+    d_land,
+    pc_sent,
+    pc_land,
+    px_sent,
+    px_land,
+    pz_sent,
+    pz_land,
+):
+    narrows = 4
+    everyone = wides * narrows
+    tok = latents.shape[0]
+    width = latents.shape[1]
+    shard = tok * narrows
+    cols = width // everyone
+    chunk = width // chunks
+    units = up.shape[2]
+    g = lax.axis_index("groups")
+    w = lax.axis_index("wide")
+    n = lax.axis_index("narrow")
+    me = w * narrows + n
+    x = n // 2
+    core = n % 2
+    over_x = (g, w, (1 - x) * 2 + core)
+    over_core = (g, w, x * 2 + 1 - core)
+    wide_of = lambda d: lax.rem(w + d, wides)
+    f32, bf16 = jnp.float32, jnp.bfloat16
+
+    load_out = pltpu.make_async_copy(out_proj_hbm, out_proj, own_sem.at[0])
+    load_up = pltpu.make_async_copy(up_hbm, up, own_sem.at[1])
+    load_down = pltpu.make_async_copy(down_hbm, down, own_sem.at[2])
+
+    barrier = pltpu.get_barrier_semaphore()
+
+    def greet(d, carry):
+        other = lax.rem(me + d, everyone)
+        pl.semaphore_signal(
+            barrier,
+            inc=1,
+            device_id=(g, other // narrows, other % narrows),
+            device_id_type=pl.DeviceIdType.MESH,
+        )
+        return carry
+
+    lax.fori_loop(1, everyone, greet, 0)
+    pl.semaphore_wait(barrier, everyone - 1)
+
+    def head_columns(other):
+        first = (other % narrows) * (wides * cols) + (other // narrows) * cols
+        return pl.ds(pl.multiple_of(first, 128), cols)
+
+    def qkv_copy(other, landing, d):
+        return copy_to(
+            proj.at[:, :, head_columns(other)],
+            qkv.at[:, landing],
+            q_sent.at[d],
+            q_land.at[landing],
+            (g, other // narrows, other % narrows),
+        )
+
+    def send_qkv(d, carry):
+        qkv_copy(lax.rem(me + d, everyone), me, d).start()
+        return carry
+
+    lax.fori_loop(1, everyone, send_qkv, 0)
+    own = pltpu.make_async_copy(
+        proj.at[:, :, head_columns(me)], qkv.at[:, me], own_sem.at[3]
+    )
+    own.start()
+
+    def table_rows(of):
+        return gates.at[pl.ds(pl.multiple_of(of * shard, shard), shard)]
+
+    def gate_copy(d, of):
+        return copy_to(
+            table, table_rows(of), t_sent.at[d], t_land.at[of], (g, wide_of(d), n)
+        )
+
+    for d in range(1, wides):
+        gate_copy(d, w).start()
+    gates[pl.ds(pl.multiple_of(w * shard, shard), shard), :] = table[...]
+    load_out.start()
+    load_up.start()
+    load_down.start()
+
+    def wait_qkv(d, carry):
+        other = lax.rem(me + d, everyone)
+        qkv_copy(other, other, d).wait_recv()
+        return carry
+
+    lax.fori_loop(1, everyone, wait_qkv, 0)
+    own.wait()
+
+    seq = everyone * tok
+    queries = qkv[0].reshape(seq, cols)
+    keys = qkv[1].reshape(seq, cols)
+    values = qkv[2].reshape(seq, cols)
+    head_of = lax.broadcasted_iota(jnp.int32, (1, cols), 1) // HEAD_DIM
+    attended = jnp.zeros((seq, cols), f32)
+    for h in range(cols // HEAD_DIM):
+        mask = jnp.where(head_of == h, 1.0, 0.0).astype(f32)
+        scores = lax.dot_general(
+            queries * mask.astype(bf16),
+            keys,
+            (((1,), (1,)), ((), ())),
+            preferred_element_type=f32,
+        ) * (HEAD_DIM ** (-0.5))
+        weights = jnp.exp(scores - jnp.max(scores, axis=1, keepdims=True))
+        total = jnp.sum(weights, axis=1, keepdims=True)
+        accum = jnp.dot(weights.astype(bf16), values, preferred_element_type=f32)
+        attended = attended + (accum / total) * mask
+    att[...] = attended.astype(bf16).reshape(wides, shard, cols)
+
+    def att_copy(d, of):
+        return copy_to(
+            att.at[wide_of(d)], att_all.at[of], a_sent.at[d], a_land.at[of], (g, wide_of(d), n)
+        )
+
+    for d in range(1, wides):
+        att_copy(d, w).start()
+    att_all[w] = att[w]
+    load_out.wait()
+    for d in range(1, wides):
+        att_copy(d, wide_of(wides - d)).wait_recv()
+
+    heads_in = jnp.concatenate([att_all[i] for i in range(wides)], axis=1)
+    part[...] = (
+        jnp.dot(heads_in, out_proj[...], preferred_element_type=f32)
+        .astype(bf16)
+        .reshape(narrows, tok, width)
+    )
+
+    def part_copy(d, of):
+        to = lax.rem(n + d, narrows)
+        return copy_to(part.at[to], part_all.at[of], b_sent.at[d], b_land.at[of], (g, w, to))
+
+    for d in (2, 1, 3):
+        part_copy(d, n).start()
+    branch = part[n].astype(f32)
+    for d in (2, 1, 3):
+        of = lax.rem(n + narrows - d, narrows)
+        part_copy(d, of).wait_recv()
+        branch = branch + part_all[of].astype(f32)
+
+    residual = latents[...].astype(f32) + modulation[0:1, :] * branch
+    res[...] = residual
+    centered = residual - jnp.mean(residual, axis=1, keepdims=True)
+    variance = jnp.mean(centered * centered, axis=1, keepdims=True)
+    normed = centered * lax.rsqrt(variance + EPSILON)
+    rows[me] = (normed * (1.0 + modulation[2:3, :]) + modulation[1:2, :]).astype(bf16)
+
+    def row_of(wide, narrow):
+        return rows.at[wide * narrows + narrow]
+
+    def z_copy(d, of):
+        return copy_to(row_of(w, n), row_of(of, n), z_sent.at[d], z_land.at[of], (g, wide_of(d), n))
+
+    def x_copy(of, narrow):
+        return copy_to(row_of(of, narrow), row_of(of, narrow), x_sent.at[of], x_land.at[of], over_x)
+
+    def c_copy(of, narrow):
+        return copy_to(
+            row_of(of, narrow), row_of(of, narrow), c_sent.at[of], c_land.at[of], over_core
+        )
+
+    def d_copy(of, narrow):
+        return copy_to(
+            row_of(of, narrow), row_of(of, narrow), d_sent.at[of], d_land.at[of], over_core
+        )
+
+    across = (1 - x) * 2 + core
+    for d in range(1, wides):
+        z_copy(d, w).start()
+    x_copy(w, n).start()
+    c_copy(w, n).start()
+    for d in range(1, wides):
+        of = wide_of(wides - d)
+        z_copy(d, of).wait_recv()
+        x_copy(of, n).start()
+        c_copy(of, n).start()
+    for d in range(wides):
+        of = wide_of(wides - d)
+        x_copy(of, across).wait_recv()
+        d_copy(of, across).start()
+    for d in range(1, wides):
+        gate_copy(d, wide_of(wides - d)).wait_recv()
+    load_up.wait()
+    for d in range(wides):
+        of = wide_of(wides - d)
+        c_copy(of, x * 2 + 1 - core).wait_recv()
+        d_copy(of, (1 - x) * 2 + 1 - core).wait_recv()
+
+    experts = up.shape[0]
+    pieces = max(1, units // 512)
+    piece = units // pieces
+    lanes = lax.broadcasted_iota(jnp.int32, (1, gates.shape[1]), 1)
+
+    def expand(step, carry):
+        e = step // pieces
+        first = pl.multiple_of((step % pieces) * piece, piece)
+        gate = jnp.sum(
+            jnp.where(lanes == w * experts + e, gates[...], 0.0), axis=1, keepdims=True
+        )
+        made = jnp.dot(
+            rows[...].reshape(seq, width),
+            up[e, :, pl.ds(first, piece)],
+            preferred_element_type=f32,
+        )
+        made = jax.nn.gelu(made, approximate=True) * gate
+        hidden[:, pl.ds(pl.multiple_of(step * piece, piece), piece)] = made.astype(bf16)
+        return carry
+
+    lax.fori_loop(0, experts * pieces, expand, 0)
+    load_down.wait()
+
+    def core_copy(c):
+        return copy_to(
+            mixed.at[c, :, :, 1 - core], core_in.at[c], pc_sent.at[c], pc_land.at[c], over_core
+        )
+
+    def pair_copy(c):
+        return copy_to(pair.at[c, :, 1 - x], x_in.at[c], px_sent.at[c], px_land.at[c], over_x)
+
+    def quad_copy(c, d, of):
+        return copy_to(
+            quad.at[c, wide_of(d)],
+            z_in.at[c, of],
+            pz_sent.at[c * wides + d],
+            pz_land.at[c * wides + of],
+            (g, wide_of(d), n),
+        )
+
+    def after_core(c):
+        core_copy(c).wait_recv()
+        total = mixed[c, :, :, core].astype(f32) + core_in[c].astype(f32)
+        pair[c] = total.astype(bf16)
+        pair_copy(c).start()
+
+    def after_x(c):
+        pair_copy(c).wait_recv()
+        quad[c] = (pair[c, :, x].astype(f32) + x_in[c].astype(f32)).astype(bf16)
+        for d in range(1, wides):
+            quad_copy(c, d, w).start()
+
+    def after_z(c):
+        total = quad[c, w].astype(f32)
+        for d in range(1, wides):
+            of = wide_of(wides - d)
+            quad_copy(c, d, of).wait_recv()
+            total = total + z_in[c, of].astype(f32)
+        at = slice(c * chunk, (c + 1) * chunk)
+        out[:, at] = (res[:, at] + modulation[3:4, at] * total).astype(bf16)
+
+    for c in range(chunks):
+        made = jnp.dot(
+            hidden[...], down[:, c * chunk : (c + 1) * chunk], preferred_element_type=f32
+        )
+        mixed[c] = made.astype(bf16).reshape(wides, 2, 2, tok, chunk)
+        core_copy(c).start()
+        if c >= 1:
+            after_core(c - 1)
+        if c >= 2:
+            after_x(c - 2)
+    after_core(chunks - 1)
+    for c in range(max(0, chunks - 2), chunks):
+        after_x(c)
+    for c in range(chunks):
+        after_z(c)
+
+    def sent_qkv(d, carry):
+        qkv_copy(lax.rem(me + d, everyone), me, d).wait_send()
+        return carry
+
+    lax.fori_loop(1, everyone, sent_qkv, 0)
+    for d in range(1, wides):
+        gate_copy(d, w).wait_send()
+        att_copy(d, w).wait_send()
+        z_copy(d, w).wait_send()
+    for d in range(1, narrows):
+        part_copy(d, n).wait_send()
+    for of in range(wides):
+        x_copy(of, n).wait_send()
+        c_copy(of, n).wait_send()
+        d_copy(of, across).wait_send()
+    for c in range(chunks):
+        core_copy(c).wait_send()
+        pair_copy(c).wait_send()
+        for d in range(1, wides):
+            quad_copy(c, d, w).wait_send()
+
+
+def fused(
+    projected, latents, modulation, routes, route_weights, out_proj, expert_up, expert_down
+):
+    wides = lax.axis_size("wide")
+    narrows = lax.axis_size("narrow")
+    tok, width = latents.shape
+    shard = tok * narrows
+    seq = shard * wides
+    cols = width // (wides * narrows)
+    experts, unused, units = expert_up.shape
+    chunks = 4
+    chunk = width // chunks
+    f32, bf16 = jnp.float32, jnp.bfloat16
+    lanes = jnp.arange(128, dtype=jnp.int32)
+    table = jnp.sum(
+        jnp.where(routes[:, :, None] == lanes[None, None, :], route_weights[:, :, None], 0.0),
+        axis=1,
+    )
+    down = expert_down.reshape(experts * units, width)
+    vmem = pl.BlockSpec(memory_space=pltpu.VMEM)
+    anywhere = pl.BlockSpec(memory_space=pl.ANY)
+    dma = pltpu.SemaphoreType.DMA
+    everyone = wides * narrows
+    sizes = [4, everyone, everyone] + [wides] * 4 + [narrows] * 2 + [wides] * 8
+    sizes += [chunks] * 4 + [chunks * wides] * 2
+    return pl.pallas_call(
+        functools.partial(block_kernel, wides, chunks),
+        out_shape=jax.ShapeDtypeStruct((tok, width), bf16),
+        in_specs=[vmem] * 4 + [anywhere] * 3,
+        out_specs=vmem,
+        scratch_shapes=[
+            pltpu.VMEM(out_proj.shape, bf16),
+            pltpu.VMEM(expert_up.shape, bf16),
+            pltpu.VMEM(down.shape, bf16),
+            pltpu.VMEM((3, everyone, tok, cols), bf16),
+            pltpu.VMEM((wides, shard, cols), bf16),
+            pltpu.VMEM((wides, shard, cols), bf16),
+            pltpu.VMEM((narrows, tok, width), bf16),
+            pltpu.VMEM((narrows, tok, width), bf16),
+            pltpu.VMEM((tok, width), f32),
+            pltpu.VMEM((everyone, tok, width), bf16),
+            pltpu.VMEM((seq, 128), f32),
+            pltpu.VMEM((seq, experts * units), bf16),
+            pltpu.VMEM((chunks, wides, 2, 2, tok, chunk), bf16),
+            pltpu.VMEM((chunks, wides, 2, tok, chunk), bf16),
+            pltpu.VMEM((chunks, wides, 2, tok, chunk), bf16),
+            pltpu.VMEM((chunks, wides, tok, chunk), bf16),
+            pltpu.VMEM((chunks, wides, tok, chunk), bf16),
+            pltpu.VMEM((chunks, wides, tok, chunk), bf16),
+        ]
+        + [dma((size,)) for size in sizes],
+        compiler_params=pltpu.CompilerParams(
+            collective_id=0, has_side_effects=True, vmem_limit_bytes=52 * 1024 * 1024
+        ),
+    )(projected, latents, modulation, table, out_proj, expert_up, down)
+
+
 def solution(mesh):
     in_specs = (
         P(None, ("groups", "wide", "narrow"), None),
@@ -116,6 +522,11 @@
         P("wide", "narrow", None),
     )
     out_specs = P(("groups", "wide", "narrow"), None)
+    small = mesh.shape["narrow"] == 4 and mesh.shape["wide"] == 4
     return jax.shard_map(
-        on_device, mesh=mesh, in_specs=in_specs, out_specs=out_specs, check_vma=False
-    )
+        fused if small else on_device,
+        mesh=mesh,
+        in_specs=in_specs,
+        out_specs=out_specs,
+        check_vma=False,
+    )

time: 196 us -> 58.4 us (0.30)
  waiting for transfers between devices: 74.6 us -> 0 us
  blocking collectives: 60 us -> 0 us
  Pallas kernels: 0 us -> 54.1 us
  local copies, waits for them, and re-layouts: 21.6 us -> 3.15 us
  between operations: 13.7 us -> 0.03 us
  matrix products: 11.5 us -> 0 us
  starting transfers between devices: 8.85 us -> 0 us
  other arithmetic: 4.91 us -> 0.79 us
    pallas_call x0 -> x1, Pallas kernels: none -> 54.1 us  [fused(): pl.pallas_call(functools.partial(block_kernel, wides, chunks), out_shape=...]
    all_gather x3 -> x0, blocking collectives: 35 us -> none  [the longest x1 14.6 us: on_device(): lax.all_gather(regrouped[1], 'wide', axis=0, tiled=True)]
    psum x1 -> x0, waiting for transfers between devices: 32.9 us -> none  [on_device(): lax.psum(partial_rows.reshape(sources, column_slots, model_width).astype(...]
    all_to_all x1 -> x0, blocking collectives: 25 us -> none  [on_device(): lax.all_to_all(bucket, 'wide', split_axis=0, concat_axis=0, tiled=True)]
    all_to_all x2 -> x0, waiting for transfers between devices: 21.5 us -> none  [the longest x1 18.8 us: on_device(): lax.all_to_all(summed, 'wide', split_axis=0, concat_axis=0, tiled=True)]
    reduce_scatter x1 -> x0, waiting for transfers between devices: 20.1 us -> none  [on_device(): lax.psum_scatter(jnp.dot(attended, out_proj, preferred_element_type=jnp.f...]
    dot_general x4 -> x0, matrix products: 11.5 us -> none  [the longest x1 9.71 us: on_device(): jnp.einsum('sjmf,jfd->sjmd', hidden_units, expert_down, preferred_element...]
    unnamed x14 -> x7, local copies, waits for them, and re-layouts: 12 us -> 3.15 us
  transfers between devices with their start and end apart: 4 -> 0, of which waited for: 4 -> 0; matrix products, arithmetic and copies ran while one was open for 2% -> 0% of each run, Pallas kernels for 0% -> 0%
where the time goes in v1:
time: 58.4 us; the launch traced here: 58.1 us
  Pallas kernels  54.1 us (93%)
  local copies, waits for them, and re-layouts  3.15 us (5%)
  other arithmetic  0.79 us (1%)
    pallas_call x1, Pallas kernels, fused(): pl.pallas_call(functools.partial(block_kernel, wides, chunks), out_shape=...  54.1 us
    unnamed x7, local copies, waits for them, and re-layouts  3.15 us

profile of v1, /device:TPU:0, one launch (start us, length us, event | category | flops | bytes accessed | tf_op | source)
XLA Modules:
  0.0 58.1 jit_solution(6778178223004644277)
XLA Ops:
  0.0 0.8 %select_reduce_fusion.table = f32[64,128]{1,0:T(8,128)S(1)} fusion(f32[64,2]{0,1:T(2,128)} %param.12, s32[64,2]{0,1:T(2,128)} %param.11), kind=kLoop, calls=%fused_computation | loop fusion | flops 40960 | bytes 33792 | tf_op jit(solution)/shard_map/reduce_sum | solution.py:470
  0.8 0.0 copy-start
  0.8 0.9 %copy-done = bf16[3,16,2048]{2,1,0:T(8,128)(2,1)S(1)} copy-done((bf16[3,16,2048]{2,1,0:T(8,128)(2,1)S(1)}, bf16[3,16,2048]{2,1,0:T(8,128)(2,1)}, u32[]{:S(2)}) %copy-start) | copy-done | bytes 196632
  1.7 0.0 copy-start.1
  1.7 0.8 %copy-done.1 = bf16[16,2048]{1,0:T(8,128)(2,1)S(1)} copy-done((bf16[16,2048]{1,0:T(8,128)(2,1)S(1)}, bf16[16,2048]{1,0:T(8,128)(2,1)}, u32[]{:S(2)}) %copy-start.1) | copy-done | bytes 65560
  2.6 0.0 copy-start.2
  2.6 0.8 %copy-done.2 = f32[4,2048]{1,0:T(4,128)S(1)} copy-done((f32[4,2048]{1,0:T(4,128)S(1)}, f32[4,2048]{1,0:T(4,128)}, u32[]{:S(2)}) %copy-start.2) | copy-done | bytes 32792
  3.3 54.1 %shard_map.82 = bf16[16,2048]{1,0:T(8,128)(2,1)S(1)} custom-call(bf16[3,16,2048]{2,1,0:T(8,128)(2,1)S(1)} %copy-done, bf16[16,2048]{1,0:T(8,128)(2,1)S(1)} %copy-done.1, f32[4,2048]{1,0:T(4,128)S(1)} %copy-done.2, f32[64,128]{1,0:T(8,128)S(1)} %select_reduce_fusion.table, bf16[512,2048]{1,0:T(8,128)(2,1)} %out_proj_hbm.1, bf16[2,2048,1024]{2,1,0:T(8,128)(2,1)} %up_hbm.1, ...), custom_call_target="tpu_custom_call" | custom-call | tf_op jit(solution)/shard_map/pallas_call | solution.py:481
  57.5 0.6 %copy.12 = bf16[16,2048]{1,0:T(8,128)(2,1)} copy(bf16[16,2048]{1,0:T(8,128)(2,1)S(1)} %shard_map.82) | data formatting | bytes 131072
Async XLA Ops:
  0.8 0.9 %copy-start = (bf16[3,16,2048]{2,1,0:T(8,128)(2,1)S(1)}, bf16[3,16,2048]{2,1,0:T(8,128)(2,1)}, u32[]{:S(2)}) copy-start(bf16[3,16,2048]{2,1,0:T(8,128)(2,1)} %proj.1) | copy-start | bytes 589828
  1.7 0.8 %copy-start.1 = (bf16[16,2048]{1,0:T(8,128)(2,1)S(1)}, bf16[16,2048]{1,0:T(8,128)(2,1)}, u32[]{:S(2)}) copy-start(bf16[16,2048]{1,0:T(8,128)(2,1)} %latents.1) | copy-start | bytes 196612
  2.6 0.8 %copy-start.2 = (f32[4,2048]{1,0:T(4,128)S(1)}, f32[4,2048]{1,0:T(4,128)}, u32[]{:S(2)}) copy-start(f32[4,2048]{1,0:T(4,128)} %modulation.1) | copy-start | bytes 98308

commit v2 on v1

--- a/solution.py
+++ b/solution.py
@@ -121,14 +121,21 @@
 def block_kernel(
     wides,
     chunks,
-    proj,
-    latents,
-    modulation,
-    table,
+    proj_hbm,
+    latents_hbm,
+    modulation_hbm,
+    routes_hbm,
+    weights_hbm,
     out_proj_hbm,
     up_hbm,
     down_hbm,
     out,
+    routes,
+    route_weights,
+    table,
+    proj,
+    latents,
+    modulation,
     out_proj,
     up,
     down,
@@ -140,6 +147,7 @@
     res,
     rows,
     gates,
+    gate_rows,
     hidden,
     mixed,
     core_in,
@@ -190,6 +198,16 @@
     wide_of = lambda d: lax.rem(w + d, wides)
     f32, bf16 = jnp.float32, jnp.bfloat16
 
+    load_proj = pltpu.make_async_copy(proj_hbm, proj, own_sem.at[4])
+    load_latents = pltpu.make_async_copy(latents_hbm, latents, own_sem.at[5])
+    load_modulation = pltpu.make_async_copy(modulation_hbm, modulation, own_sem.at[6])
+    load_proj.start()
+    load_latents.start()
+    load_modulation.start()
+    load_routes = pltpu.make_async_copy(routes_hbm, routes, own_sem.at[7])
+    load_weights = pltpu.make_async_copy(weights_hbm, route_weights, own_sem.at[8])
+    load_routes.start()
+    load_weights.start()
     load_out = pltpu.make_async_copy(out_proj_hbm, out_proj, own_sem.at[0])
     load_up = pltpu.make_async_copy(up_hbm, up, own_sem.at[1])
     load_down = pltpu.make_async_copy(down_hbm, down, own_sem.at[2])
@@ -208,6 +226,7 @@
 
     lax.fori_loop(1, everyone, greet, 0)
     pl.semaphore_wait(barrier, everyone - 1)
+    load_proj.wait()
 
     def head_columns(other):
         first = (other % narrows) * (wides * cols) + (other // narrows) * cols
@@ -232,17 +251,20 @@
     )
     own.start()
 
-    def table_rows(of):
-        return gates.at[pl.ds(pl.multiple_of(of * shard, shard), shard)]
-
     def gate_copy(d, of):
-        return copy_to(
-            table, table_rows(of), t_sent.at[d], t_land.at[of], (g, wide_of(d), n)
-        )
+        return copy_to(table, gates.at[of], t_sent.at[d], t_land.at[of], (g, wide_of(d), n))
+
+    load_routes.wait()
+    load_weights.wait()
+    named = lax.broadcasted_iota(jnp.int32, (table.shape[0], shard), 0)
+    table[:, :shard] = jnp.where(named == routes[0:1, :], route_weights[0:1, :], 0.0) + jnp.where(
+        named == routes[1:2, :], route_weights[1:2, :], 0.0
+    )
+    table[:, shard:] = jnp.zeros((table.shape[0], table.shape[1] - shard), f32)
 
     for d in range(1, wides):
         gate_copy(d, w).start()
-    gates[pl.ds(pl.multiple_of(w * shard, shard), shard), :] = table[...]
+    gates[w] = table[...]
     load_out.start()
     load_up.start()
     load_down.start()
@@ -300,6 +322,8 @@
 
     for d in (2, 1, 3):
         part_copy(d, n).start()
+    load_latents.wait()
+    load_modulation.wait()
     branch = part[n].astype(f32)
     for d in (2, 1, 3):
         of = lax.rem(n + narrows - d, narrows)
@@ -338,43 +362,68 @@
     x_copy(w, n).start()
     c_copy(w, n).start()
     for d in range(1, wides):
+        gate_copy(d, wide_of(wides - d)).wait_recv()
+    experts = up.shape[0]
+    which = lax.broadcasted_iota(jnp.int32, (table.shape[0], 1), 0)
+    for e in range(experts):
+        for of in range(wides):
+            line = jnp.sum(
+                jnp.where(which == w * experts + e, gates[of], 0.0), axis=0, keepdims=True
+            )
+            square = jnp.broadcast_to(line, (line.shape[1], line.shape[1])).T
+            gate_rows[e, of * shard : (of + 1) * shard, :] = square[:shard, :]
+    for d in range(1, wides):
         of = wide_of(wides - d)
         z_copy(d, of).wait_recv()
         x_copy(of, n).start()
         c_copy(of, n).start()
-    for d in range(wides):
+    def cross(d):
         of = wide_of(wides - d)
         x_copy(of, across).wait_recv()
         d_copy(of, across).start()
-    for d in range(1, wides):
-        gate_copy(d, wide_of(wides - d)).wait_recv()
-    load_up.wait()
-    for d in range(wides):
+
+    def gathered(d):
         of = wide_of(wides - d)
         c_copy(of, x * 2 + 1 - core).wait_recv()
         d_copy(of, (1 - x) * 2 + 1 - core).wait_recv()
 
-    experts = up.shape[0]
     pieces = max(1, units // 512)
     piece = units // pieces
-    lanes = lax.broadcasted_iota(jnp.int32, (1, gates.shape[1]), 1)
-
-    def expand(step, carry):
+    steps = experts * pieces
+
+    def expand(shards, step, carry):
         e = step // pieces
         first = pl.multiple_of((step % pieces) * piece, piece)
-        gate = jnp.sum(
-            jnp.where(lanes == w * experts + e, gates[...], 0.0), axis=1, keepdims=True
-        )
+        taken = [rows[pl.ds(of * narrows, narrows)].reshape(shard, width) for of in shards]
         made = jnp.dot(
-            rows[...].reshape(seq, width),
+            jnp.concatenate(taken, axis=0),
             up[e, :, pl.ds(first, piece)],
             preferred_element_type=f32,
         )
-        made = jax.nn.gelu(made, approximate=True) * gate
-        hidden[:, pl.ds(pl.multiple_of(step * piece, piece), piece)] = made.astype(bf16)
+        made = jax.nn.gelu(made, approximate=True)
+        columns = pl.ds(pl.multiple_of(step * piece, piece), piece)
+        for k, of in enumerate(shards):
+            lines = pl.ds(pl.multiple_of(of * shard, shard), shard)
+            scaled = made[k * shard : (k + 1) * shard] * gate_rows[e, lines, 0:1]
+            hidden[lines, columns] = scaled.astype(bf16)
         return carry
 
-    lax.fori_loop(0, experts * pieces, expand, 0)
+    half = wides // 2
+    near = [wide_of(wides - d) for d in range(half)]
+    far = [wide_of(wides - d) for d in range(half, wides)]
+    for d in range(half):
+        cross(d)
+    load_up.wait()
+    for d in range(half):
+        gathered(d)
+    lax.fori_loop(0, steps // 2, functools.partial(expand, near), 0)
+    cross(half)
+    lax.fori_loop(steps // 2, steps, functools.partial(expand, near), 0)
+    for d in range(half + 1, wides):
+        cross(d)
+    for d in range(half, wides):
+        gathered(d)
+    lax.fori_loop(0, steps, functools.partial(expand, far), 0)
     load_down.wait()
 
     def core_copy(c):
@@ -423,10 +472,8 @@
         core_copy(c).start()
         if c >= 1:
             after_core(c - 1)
-        if c >= 2:
-            after_x(c - 2)
     after_core(chunks - 1)
-    for c in range(max(0, chunks - 2), chunks):
+    for c in range(chunks):
         after_x(c)
     for c in range(chunks):
         after_z(c)
@@ -466,24 +513,25 @@
     chunks = 4
     chunk = width // chunks
     f32, bf16 = jnp.float32, jnp.bfloat16
-    lanes = jnp.arange(128, dtype=jnp.int32)
-    table = jnp.sum(
-        jnp.where(routes[:, :, None] == lanes[None, None, :], route_weights[:, :, None], 0.0),
-        axis=1,
-    )
     down = expert_down.reshape(experts * units, width)
     vmem = pl.BlockSpec(memory_space=pltpu.VMEM)
-    anywhere = pl.BlockSpec(memory_space=pl.ANY)
+    hbm = pl.BlockSpec(memory_space=pltpu.HBM)
     dma = pltpu.SemaphoreType.DMA
     everyone = wides * narrows
-    sizes = [4, everyone, everyone] + [wides] * 4 + [narrows] * 2 + [wides] * 8
+    sizes = [9, everyone, everyone] + [wides] * 4 + [narrows] * 2 + [wides] * 8
     sizes += [chunks] * 4 + [chunks * wides] * 2
     return pl.pallas_call(
         functools.partial(block_kernel, wides, chunks),
         out_shape=jax.ShapeDtypeStruct((tok, width), bf16),
-        in_specs=[vmem] * 4 + [anywhere] * 3,
+        in_specs=[hbm] * 8,
         out_specs=vmem,
         scratch_shapes=[
+            pltpu.VMEM((2, shard), jnp.int32),
+            pltpu.VMEM((2, shard), f32),
+            pltpu.VMEM((experts * wides, 128), f32),
+            pltpu.VMEM(projected.shape, bf16),
+            pltpu.VMEM((tok, width), bf16),
+            pltpu.VMEM(modulation.shape, f32),
             pltpu.VMEM(out_proj.shape, bf16),
             pltpu.VMEM(expert_up.shape, bf16),
             pltpu.VMEM(down.shape, bf16),
@@ -494,7 +542,8 @@
             pltpu.VMEM((narrows, tok, width), bf16),
             pltpu.VMEM((tok, width), f32),
             pltpu.VMEM((everyone, tok, width), bf16),
-            pltpu.VMEM((seq, 128), f32),
+            pltpu.VMEM((wides, experts * wides, 128), f32),
+            pltpu.VMEM((experts, seq, 128), f32),
             pltpu.VMEM((seq, experts * units), bf16),
             pltpu.VMEM((chunks, wides, 2, 2, tok, chunk), bf16),
             pltpu.VMEM((chunks, wides, 2, tok, chunk), bf16),
@@ -507,7 +556,7 @@
         compiler_params=pltpu.CompilerParams(
             collective_id=0, has_side_effects=True, vmem_limit_bytes=52 * 1024 * 1024
         ),
-    )(projected, latents, modulation, table, out_proj, expert_up, down)
+    )(projected, latents, modulation, routes.T, route_weights.T, out_proj, expert_up, down)
 
 
 def solution(mesh):

time: 58.4 us -> 57 us (0.976)
  Pallas kernels: 54.1 us -> 52.2 us
  local copies, waits for them, and re-layouts: 3.15 us -> 4.51 us
  other arithmetic: 0.79 us -> 0 us
    pallas_call x1, Pallas kernels: 54.1 us -> 52.2 us  [fused(): pl.pallas_call(functools.partial(block_kernel, wides, chunks), out_shape=...]
    unnamed x7 -> x11, local copies, waits for them, and re-layouts: 3.15 us -> 4.51 us
    reduce_sum x1 -> x0, other arithmetic: 0.79 us -> none  [fused(): jnp.sum(jnp.where(routes[:, :, None] == lanes[None, None, :], route_weigh...]
where the time goes in v2:
time: 57 us; the launch traced here: 56.7 us
  Pallas kernels  52.2 us (92%)
  local copies, waits for them, and re-layouts  4.51 us (8%)
    pallas_call x1, Pallas kernels, fused(): pl.pallas_call(functools.partial(block_kernel, wides, chunks), out_shape=...  52.2 us
    unnamed x11, local copies, waits for them, and re-layouts  4.51 us

profile of v2, /device:TPU:0, one launch (start us, length us, event | category | flops | bytes accessed | tf_op | source)
XLA Modules:
  0.0 56.7 jit_solution(515401171226912526)
XLA Ops:
  0.0 0.0 copy-start
  0.0 0.9 %copy-done = bf16[3,16,2048]{2,1,0:T(8,128)(2,1)S(1)} copy-done((bf16[3,16,2048]{2,1,0:T(8,128)(2,1)S(1)}, bf16[3,16,2048]{2,1,0:T(8,128)(2,1)}, u32[]{:S(2)}) %copy-start) | copy-done | bytes 196632
  0.9 0.0 copy-start.1
  0.9 0.8 %copy-done.1 = bf16[16,2048]{1,0:T(8,128)(2,1)S(1)} copy-done((bf16[16,2048]{1,0:T(8,128)(2,1)S(1)}, bf16[16,2048]{1,0:T(8,128)(2,1)}, u32[]{:S(2)}) %copy-start.1) | copy-done | bytes 65560
  1.8 0.0 copy-start.2
  1.8 0.8 %copy-done.2 = f32[4,2048]{1,0:T(4,128)S(1)} copy-done((f32[4,2048]{1,0:T(4,128)S(1)}, f32[4,2048]{1,0:T(4,128)}, u32[]{:S(2)}) %copy-start.2) | copy-done | bytes 32792
  2.5 0.0 copy-start.3
  2.5 0.7 %copy-done.3 = s32[64,2]{0,1:T(2,128)S(1)} copy-done((s32[64,2]{0,1:T(2,128)S(1)}, s32[64,2]{0,1:T(2,128)}, u32[]{:S(2)}) %copy-start.3) | copy-done | bytes 536
  3.2 0.0 copy-start.4
  3.2 0.7 %copy-done.4 = f32[64,2]{0,1:T(2,128)S(1)} copy-done((f32[64,2]{0,1:T(2,128)S(1)}, f32[64,2]{0,1:T(2,128)}, u32[]{:S(2)}) %copy-start.4) | copy-done | bytes 536
  3.9 52.2 %shard_map.82 = bf16[16,2048]{1,0:T(8,128)(2,1)S(1)} custom-call(bf16[3,16,2048]{2,1,0:T(8,128)(2,1)S(1)} %copy-done, bf16[16,2048]{1,0:T(8,128)(2,1)S(1)} %copy-done.1, f32[4,2048]{1,0:T(4,128)S(1)} %copy-done.2, s32[2,64]{1,0:T(2,128)S(1)} %bitcast.3, f32[2,64]{1,0:T(2,128)S(1)} %bitcast.4, bf16[512,2048]{1,0:T(8,128)(2,1)} %out_proj_hbm.1, ...), custom_call_target="tpu_custom_call" | custom-call | tf_op jit(solution)/shard_map/pallas_call | solution.py:523
  56.1 0.6 %copy.10 = bf16[16,2048]{1,0:T(8,128)(2,1)} copy(bf16[16,2048]{1,0:T(8,128)(2,1)S(1)} %shard_map.82) | data formatting | bytes 131072
Async XLA Ops:
  0.0 0.9 %copy-start = (bf16[3,16,2048]{2,1,0:T(8,128)(2,1)S(1)}, bf16[3,16,2048]{2,1,0:T(8,128)(2,1)}, u32[]{:S(2)}) copy-start(bf16[3,16,2048]{2,1,0:T(8,128)(2,1)} %proj_hbm.1) | copy-start | bytes 589828
  0.9 0.8 %copy-start.1 = (bf16[16,2048]{1,0:T(8,128)(2,1)S(1)}, bf16[16,2048]{1,0:T(8,128)(2,1)}, u32[]{:S(2)}) copy-start(bf16[16,2048]{1,0:T(8,128)(2,1)} %latents_hbm.1) | copy-start | bytes 196612
  1.8 0.8 %copy-start.2 = (f32[4,2048]{1,0:T(4,128)S(1)}, f32[4,2048]{1,0:T(4,128)}, u32[]{:S(2)}) copy-start(f32[4,2048]{1,0:T(4,128)} %modulation_hbm.1) | copy-start | bytes 98308
  2.5 0.7 %copy-start.3 = (s32[64,2]{0,1:T(2,128)S(1)}, s32[64,2]{0,1:T(2,128)}, u32[]{:S(2)}) copy-start(s32[64,2]{0,1:T(2,128)} %param.11) | copy-start | bytes 1540
  3.2 0.7 %copy-start.4 = (f32[64,2]{0,1:T(2,128)S(1)}, f32[64,2]{0,1:T(2,128)}, u32[]{:S(2)}) copy-start(f32[64,2]{0,1:T(2,128)} %param.12) | copy-start | bytes 1540

commit v3 on v2

--- a/solution.py
+++ b/solution.py
@@ -554,7 +554,7 @@
         ]
         + [dma((size,)) for size in sizes],
         compiler_params=pltpu.CompilerParams(
-            collective_id=0, has_side_effects=True, vmem_limit_bytes=52 * 1024 * 1024
+            collective_id=0, has_side_effects=True, vmem_limit_bytes=65400 * 1024
         ),
     )(projected, latents, modulation, routes.T, route_weights.T, out_proj, expert_up, down)
 

time: 57 us -> 54 us (0.947)
  local copies, waits for them, and re-layouts: 4.51 us -> 1.47 us
    unnamed x11 -> x1, local copies, waits for them, and re-layouts: 4.51 us -> 1.47 us
where the time goes in v3:
time: 54 us; the launch traced here: 53.8 us
  Pallas kernels  52.4 us (97%)
  local copies, waits for them, and re-layouts  1.47 us (3%)
    pallas_call x1, Pallas kernels, fused(): pl.pallas_call(functools.partial(block_kernel, wides, chunks), out_shape=...  52.4 us
    unnamed x1, local copies, waits for them, and re-layouts  1.47 us

profile of v3, /device:TPU:0, one launch (start us, length us, event | category | flops | bytes accessed | tf_op | source)
XLA Modules:
  0.0 53.8 jit_solution(15405218259302297282)
XLA Ops:
  0.0 52.4 %shard_map.82 = bf16[16,2048]{1,0:T(8,128)(2,1)} custom-call(bf16[3,16,2048]{2,1,0:T(8,128)(2,1)} %proj_hbm.1, bf16[16,2048]{1,0:T(8,128)(2,1)} %latents_hbm.1, f32[4,2048]{1,0:T(4,128)} %modulation_hbm.1, s32[2,64]{1,0:T(2,128)} %bitcast.4, f32[2,64]{1,0:T(2,128)} %bitcast.5, bf16[512,2048]{1,0:T(8,128)(2,1)} %out_proj_hbm.1, ...), custom_call_target="tpu_custom_call" | custom-call | tf_op jit(solution)/shard_map/pallas_call | solution.py:523
  52.4 1.5 %copy.10 = bf16[16,2048]{1,0:T(8,128)(2,1)} copy(bf16[16,2048]{1,0:T(8,128)(2,1)} %shard_map.82) | data formatting | bytes 131072

commit v4 on v3

--- a/solution.py
+++ b/solution.py
@@ -211,6 +211,9 @@
     load_out = pltpu.make_async_copy(out_proj_hbm, out_proj, own_sem.at[0])
     load_up = pltpu.make_async_copy(up_hbm, up, own_sem.at[1])
     load_down = pltpu.make_async_copy(down_hbm, down, own_sem.at[2])
+    load_out.start()
+    load_up.start()
+    load_down.start()
 
     barrier = pltpu.get_barrier_semaphore()
 
@@ -265,9 +268,6 @@
     for d in range(1, wides):
         gate_copy(d, w).start()
     gates[w] = table[...]
-    load_out.start()
-    load_up.start()
-    load_down.start()
 
     def wait_qkv(d, carry):
         other = lax.rem(me + d, everyone)

time: 54 us -> 54.1 us (level)
  no operation moved by 1% of the time
where the time goes in v4:
time: 54.1 us; the launch traced here: 53.9 us
  Pallas kernels  52.4 us (97%)
  local copies, waits for them, and re-layouts  1.47 us (3%)
    pallas_call x1, Pallas kernels, fused(): pl.pallas_call(functools.partial(block_kernel, wides, chunks), out_shape=...  52.4 us
    unnamed x1, local copies, waits for them, and re-layouts  1.47 us

profile of v4, /device:TPU:0, one launch (start us, length us, event | category | flops | bytes accessed | tf_op | source)
XLA Modules:
  0.0 53.9 jit_solution(5994791815150810283)
XLA Ops:
  0.0 52.4 %shard_map.82 = bf16[16,2048]{1,0:T(8,128)(2,1)} custom-call(bf16[3,16,2048]{2,1,0:T(8,128)(2,1)} %proj_hbm.1, bf16[16,2048]{1,0:T(8,128)(2,1)} %latents_hbm.1, f32[4,2048]{1,0:T(4,128)} %modulation_hbm.1, s32[2,64]{1,0:T(2,128)} %bitcast.4, f32[2,64]{1,0:T(2,128)} %bitcast.5, bf16[512,2048]{1,0:T(8,128)(2,1)} %out_proj_hbm.1, ...), custom_call_target="tpu_custom_call" | custom-call | tf_op jit(solution)/shard_map/pallas_call | solution.py:523
  52.4 1.5 %copy.10 = bf16[16,2048]{1,0:T(8,128)(2,1)} copy(bf16[16,2048]{1,0:T(8,128)(2,1)} %shard_map.82) | data formatting | bytes 131072
